TPU v7x, 128 devices: a whole 4x4x4 slice. The times are simulated.
128 devices in a mesh: exp: 64 (over y_lo, x, z, core), rep: 2 (over y_hi).
Axes of the slice: x: 4, y: 4 (y_hi: 2, y_lo: 2; y = y_hi * 2 + y_lo), z: 4, core: 2. Of those that a mesh axis runs over, the one named last changes fastest.
Arguments:
- tokens: bfloat16 [768, 256, 1280], P(('exp', 'rep')), may hold values from -6 to 6
- out_grad: bfloat16 [768, 256, 1280], P(('exp', 'rep')), may hold values from -12 to 12
- router: bfloat16 [64, 1280], replicated, may hold values from -1 to 1
- w_in: bfloat16 [64, 1280, 2560], P('exp'), may hold values from -0.15625 to 0.15625
- w_out: bfloat16 [64, 2560, 1280], P('exp'), may hold values from -0.125 to 0.125
Outputs:
- token_grad: bfloat16 [768, 256, 1280], P(('exp', 'rep'))
- w_in_grad: bfloat16 [64, 1280, 2560], P('exp', None, 'rep')
- w_out_grad: bfloat16 [64, 2560, 1280], P('exp', 'rep')
- router_grad: float32 [64, 1280], replicated
All inputs are finite; a program needn't handle non-finite values.
Results may differ from a plain program's by a relative error of at most 0.02.
Values may be sent and summed in bfloat16 or wider, within the bound.
No kernel may reach another device: no remote copies, remote signals or barrier semaphores. Data moves between devices by JAX's collectives and lax.ppermute only.
A program may use at most 192 MiB of HBM per device.

v0:
```python
import functools

import jax
import jax.numpy as jnp
from jax import lax
from jax.experimental import pallas as pl
from jax.experimental.pallas import tpu as pltpu
from jax.sharding import PartitionSpec as P

BF16, F32 = jnp.bfloat16, jnp.float32
NN, NT, TN = ((1,), (0,)), ((1,), (1,)), ((0,), (0,))
VMEM_LIMIT = 56 * 2**20
LANES = 128


def mm(a, b, dims):
    return lax.dot_general(a, b, (dims, ((), ())), preferred_element_type=F32)


def params():
    return pltpu.CompilerParams(vmem_limit_bytes=VMEM_LIMIT)


def gelu_parts(hidden):
    cdf = 0.5 * (1.0 + lax.erf(hidden * 0.7071067811865476))
    density = jnp.exp(-0.5 * hidden * hidden) * 0.3989422804014327
    return hidden * cdf, cdf + hidden * density


def stage_rows(packed_ref, stage_ref):
    groups, rows, _ = packed_ref.shape

    def body(g, carry):
        stage_ref[pl.ds(g, rows, stride=groups), :] = packed_ref[g].astype(F32)
        return carry

    lax.fori_loop(0, groups, body, 0, unroll=8)


def pack_rows(stage_ref, packed_ref):
    groups, rows, _ = packed_ref.shape

    def body(g, carry):
        packed_ref[g] = stage_ref[pl.ds(g, rows, stride=groups), :].astype(BF16)
        return carry

    lax.fori_loop(0, groups, body, 0, unroll=8)


def piece_rows(piece, which, first, count, images, groups):
    start = ((piece * 2 + which) * images + first) * groups
    return pl.ds(start if isinstance(start, int) else pl.multiple_of(start, groups), count * groups)


def whole_rows(stage_ref, which, first, count, images, groups):
    pieces = stage_ref.shape[0] // (2 * images * groups)
    parts = [stage_ref[piece_rows(p, which, first, count, images, groups), :] for p in range(pieces)]
    return jnp.concatenate([part.astype(BF16) for part in parts], axis=1)


def put_rows(stage_ref, value, which, first, count, images, groups):
    for p in range(value.shape[1] // LANES):
        cols = value[:, p * LANES : (p + 1) * LANES]
        stage_ref[piece_rows(p, which, first, count, images, groups), :] = cols


def gather_body(images, tokens_ref, grad_ref, router_ref, disp_ref, comb_ref, packed_ref, stage_ref):
    i = pl.program_id(0)
    slots = router_ref.shape[0]
    tok = tokens_ref[0]
    logits = mm(router_ref[...], tok, NT)
    d_exp = jnp.exp(logits - jnp.max(logits, axis=1, keepdims=True))
    dispatch = d_exp / jnp.sum(d_exp, axis=1, keepdims=True)
    c_exp = jnp.exp(logits - jnp.max(logits, axis=0, keepdims=True))
    combine = c_exp / jnp.sum(c_exp, axis=0, keepdims=True)
    disp_ref[0] = dispatch
    comb_ref[0] = combine
    slot_in = mm(dispatch.astype(BF16), tok, NN)
    slot_grad = mm(combine.astype(BF16), grad_ref[0], NN)
    put_rows(stage_ref, slot_in, 0, i, 1, images, slots)
    put_rows(stage_ref, slot_grad, 1, i, 1, images, slots)

    @pl.when(i == images - 1)
    def _():
        pack_rows(stage_ref, packed_ref)


def gather_slots(tokens, out_grad, router):
    images, toks, width = tokens.shape
    slots = router.shape[0]
    packed = (slots, 2 * images * width // LANES, LANES)
    image = lambda i: (i, 0, 0)
    return pl.pallas_call(
        functools.partial(gather_body, images),
        grid=(images,),
        in_specs=[
            pl.BlockSpec((1, toks, width), image),
            pl.BlockSpec((1, toks, width), image),
            pl.BlockSpec((slots, width), lambda i: (0, 0)),
        ],
        out_specs=[
            pl.BlockSpec((1, slots, toks), image),
            pl.BlockSpec((1, slots, toks), image),
            pl.BlockSpec(packed, lambda i: (0, 0, 0)),
        ],
        out_shape=[
            jax.ShapeDtypeStruct((images, slots, toks), F32),
            jax.ShapeDtypeStruct((images, slots, toks), F32),
            jax.ShapeDtypeStruct(packed, BF16),
        ],
        scratch_shapes=[pltpu.VMEM((packed[0] * packed[1], LANES), F32)],
        compiler_params=params(),
        name="gather_slots",
    )(tokens, out_grad, router)


def expert_body(images, packed_ref, w_in_ref, w_out_ref, act_ref, dhid_ref, back_ref,
                stage_ref, in_ref, grad_ref, out_acc, back_acc):
    f = pl.program_id(0)
    groups = packed_ref.shape[0]

    @pl.when(f == 0)
    def _():
        stage_rows(packed_ref, stage_ref)
        in_ref[...] = whole_rows(stage_ref, 0, 0, images, images, groups)
        grad_ref[...] = whole_rows(stage_ref, 1, 0, images, images, groups)

    w_in, w_out = w_in_ref[0], w_out_ref[0]
    act, slope = gelu_parts(mm(in_ref[...], w_in, NN))
    act = act.astype(BF16)
    act_ref[...] = act
    dhid = (mm(grad_ref[...], w_out, NT) * slope).astype(BF16)
    dhid_ref[...] = dhid
    row_out = mm(act, w_out, NN)
    row_back = mm(dhid, w_in, NT)

    @pl.when(f == 0)
    def _():
        out_acc[...] = row_out
        back_acc[...] = row_back

    @pl.when(f > 0)
    def _():
        out_acc[...] += row_out
        back_acc[...] += row_back

    @pl.when(f == pl.num_programs(0) - 1)
    def _():
        put_rows(stage_ref, out_acc[...], 0, 0, images, images, groups)
        put_rows(stage_ref, back_acc[...], 1, 0, images, images, groups)
        pack_rows(stage_ref, back_ref)


def experts(packed, w_in, w_out, block):
    width, hidden = w_in.shape[1:]
    groups = packed.shape[0]
    rows = packed.shape[1] * LANES // (2 * width) * groups
    return pl.pallas_call(
        functools.partial(expert_body, rows // groups),
        grid=(hidden // block,),
        in_specs=[
            pl.BlockSpec(packed.shape, lambda f: (0, 0, 0)),
            pl.BlockSpec((1, width, block), lambda f: (0, 0, f)),
            pl.BlockSpec((1, block, width), lambda f: (0, f, 0)),
        ],
        out_specs=[
            pl.BlockSpec((rows, block), lambda f: (0, f)),
            pl.BlockSpec((rows, block), lambda f: (0, f)),
            pl.BlockSpec(packed.shape, lambda f: (0, 0, 0)),
        ],
        out_shape=[
            jax.ShapeDtypeStruct((rows, hidden), BF16),
            jax.ShapeDtypeStruct((rows, hidden), BF16),
            jax.ShapeDtypeStruct(packed.shape, BF16),
        ],
        scratch_shapes=[
            pltpu.VMEM((groups * packed.shape[1], LANES), F32),
            pltpu.VMEM((rows, width), BF16),
            pltpu.VMEM((rows, width), BF16),
            pltpu.VMEM((rows, width), F32),
            pltpu.VMEM((rows, width), F32),
        ],
        compiler_params=params(),
        name="experts",
    )(packed, w_in, w_out)


def logit_body(images, packed_ref, tokens_ref, grad_ref, disp_ref, comb_ref, lgrad_ref, sback_ref, router_ref,
               stage_ref, acc_ref):
    i = pl.program_id(0)
    slots = packed_ref.shape[0]

    @pl.when(i == 0)
    def _():
        stage_rows(packed_ref, stage_ref)

    slot_out = whole_rows(stage_ref, 0, i, 1, images, slots)
    slot_back = whole_rows(stage_ref, 1, i, 1, images, slots)
    sback_ref[0] = slot_back
    tok = tokens_ref[0]
    comb_dot = mm(slot_out, grad_ref[0], NT)
    disp_dot = mm(slot_back, tok, NT)
    combine, dispatch = comb_ref[0], disp_ref[0]
    comb_part = combine * (comb_dot - jnp.sum(combine * comb_dot, axis=0, keepdims=True))
    disp_part = dispatch * (disp_dot - jnp.sum(dispatch * disp_dot, axis=1, keepdims=True))
    lgrad = (comb_part + disp_part).astype(BF16)
    lgrad_ref[0] = lgrad
    part = mm(lgrad, tok, NN)

    @pl.when(i == 0)
    def _():
        acc_ref[...] = part

    @pl.when(i > 0)
    def _():
        acc_ref[...] += part

    @pl.when(i == images - 1)
    def _():
        router_ref[...] = acc_ref[...].astype(BF16)


def logit_grads(packed, tokens, out_grad, dispatch, combine):
    images, toks, width = tokens.shape
    slots = packed.shape[0]
    image = lambda i: (i, 0, 0)
    return pl.pallas_call(
        functools.partial(logit_body, images),
        grid=(images,),
        in_specs=[
            pl.BlockSpec(packed.shape, lambda i: (0, 0, 0)),
            pl.BlockSpec((1, toks, width), image),
            pl.BlockSpec((1, toks, width), image),
            pl.BlockSpec((1, slots, toks), image),
            pl.BlockSpec((1, slots, toks), image),
        ],
        out_specs=[
            pl.BlockSpec((1, slots, toks), image),
            pl.BlockSpec((1, slots, width), image),
            pl.BlockSpec((slots, width), lambda i: (0, 0)),
        ],
        out_shape=[
            jax.ShapeDtypeStruct((images, slots, toks), BF16),
            jax.ShapeDtypeStruct((images, slots, width), BF16),
            jax.ShapeDtypeStruct((slots, width), BF16),
        ],
        scratch_shapes=[
            pltpu.VMEM((slots * packed.shape[1], LANES), F32),
            pltpu.VMEM((slots, width), F32),
        ],
        compiler_params=params(),
        name="logit_grads",
    )(packed, tokens, out_grad, dispatch, combine)


def token_body(lgrad_ref, disp_ref, sback_ref, router_ref, out_ref):
    left = jnp.concatenate([lgrad_ref[0], disp_ref[0].astype(BF16)], axis=0)
    right = jnp.concatenate([router_ref[...], sback_ref[0]], axis=0)
    out_ref[0] = mm(left, right, TN).astype(BF16)


def token_grads(lgrad, dispatch, slot_back, router):
    images, slots, toks = lgrad.shape
    width = router.shape[1]
    image = lambda i: (i, 0, 0)
    return pl.pallas_call(
        token_body,
        grid=(images,),
        in_specs=[
            pl.BlockSpec((1, slots, toks), image),
            pl.BlockSpec((1, slots, toks), image),
            pl.BlockSpec((1, slots, width), image),
            pl.BlockSpec((slots, width), lambda i: (0, 0)),
        ],
        out_specs=pl.BlockSpec((1, toks, width), image),
        out_shape=jax.ShapeDtypeStruct((images, toks, width), BF16),
        compiler_params=params(),
        name="token_grads",
    )(lgrad, dispatch, slot_back, router)


def weight_body(images, start_ref, own_ref, peer_ref, w_in_ref, w_out_ref, act_ref, dhid_ref,
                gin_ref, gout_ref, stage_ref, in_ref, grad_ref):
    del start_ref
    f = pl.program_id(0)
    groups = own_ref.shape[0]
    rows = images * groups

    @pl.when(f == 0)
    def _():
        for part, packed_ref in enumerate((own_ref, peer_ref)):
            stage_rows(packed_ref, stage_ref)
            where = pl.ds(part * rows, rows)
            in_ref[where, :] = whole_rows(stage_ref, 0, 0, images, images, groups)
            grad_ref[where, :] = whole_rows(stage_ref, 1, 0, images, images, groups)

    act, slope = gelu_parts(mm(in_ref[rows:, :], w_in_ref[0], NN))
    dhid = (mm(grad_ref[rows:, :], w_out_ref[0], NT) * slope).astype(BF16)
    act = jnp.concatenate([act_ref[...], act.astype(BF16)], axis=0)
    dhid = jnp.concatenate([dhid_ref[...], dhid], axis=0)
    gin_ref[0] = mm(in_ref[...], dhid, TN).astype(BF16)
    gout_ref[0] = mm(act, grad_ref[...], TN).astype(BF16)


def weight_grads(start, own, peer, w_in, w_out, act, dhid, block, reps):
    width, hidden = w_in.shape[1], w_in.shape[2] // reps
    groups = own.shape[0]
    rows = own.shape[1] * LANES // (2 * width) * groups
    return pl.pallas_call(
        functools.partial(weight_body, rows // groups),
        grid_spec=pltpu.PrefetchScalarGridSpec(
            num_scalar_prefetch=1,
            grid=(hidden // block,),
            in_specs=[
                pl.BlockSpec(own.shape, lambda f, s: (0, 0, 0)),
                pl.BlockSpec(own.shape, lambda f, s: (0, 0, 0)),
                pl.BlockSpec((1, width, block), lambda f, s: (0, 0, s[0] + f)),
                pl.BlockSpec((1, block, width), lambda f, s: (0, s[0] + f, 0)),
                pl.BlockSpec((rows, block), lambda f, s: (0, s[0] + f)),
                pl.BlockSpec((rows, block), lambda f, s: (0, s[0] + f)),
            ],
            out_specs=[
                pl.BlockSpec((1, width, block), lambda f, s: (0, 0, f)),
                pl.BlockSpec((1, block, width), lambda f, s: (0, f, 0)),
            ],
            scratch_shapes=[
                pltpu.VMEM((groups * own.shape[1], LANES), F32),
                pltpu.VMEM((2 * rows, width), BF16),
                pltpu.VMEM((2 * rows, width), BF16),
            ],
        ),
        out_shape=[
            jax.ShapeDtypeStruct((1, width, hidden), BF16),
            jax.ShapeDtypeStruct((1, hidden, width), BF16),
        ],
        compiler_params=params(),
        name="weight_grads",
    )(start, own, peer, w_in, w_out, act, dhid)


def swap(value, axis):
    return lax.all_to_all(value, axis, split_axis=0, concat_axis=0, tiled=True)


def per_device(tokens, out_grad, router, w_in, w_out):
    reps = lax.axis_size("rep")
    devices = lax.axis_size("exp") * reps
    dispatch, combine, to_experts = gather_slots(tokens, out_grad, router)
    own = swap(to_experts, "exp")
    act, dhid, to_images = experts(own, w_in, w_out, 512)
    peer = lax.ppermute(own, "rep", [(i, i ^ 1) for i in range(reps)])
    back = swap(to_images, "exp")
    lgrad, slot_back, router_part = logit_grads(back, tokens, out_grad, dispatch, combine)
    shares = swap(router_part.reshape(devices, -1, 128), ("exp", "rep")).astype(F32)
    share = jnp.sum(shares, axis=0).astype(BF16)
    router_grad = swap(jnp.broadcast_to(share[None], shares.shape), ("exp", "rep"))
    router_grad = router_grad.reshape(router.shape).astype(F32)
    token_grad = token_grads(lgrad, dispatch, slot_back, router)
    block = 256
    start = (lax.axis_index("rep") * (w_in.shape[2] // reps // block)).astype(jnp.int32).reshape(1)
    grad_in, grad_out = weight_grads(start, own, peer, w_in, w_out, act, dhid, block, reps)
    return token_grad, grad_in, grad_out, router_grad


def solution(mesh):
    in_specs = (
        P(("exp", "rep"), None, None),
        P(("exp", "rep"), None, None),
        P(),
        P("exp", None, None),
        P("exp", None, None),
    )
    out_specs = (P(("exp", "rep"), None, None), P("exp", None, "rep"), P("exp", "rep", None), P())
    return jax.shard_map(
        per_device, mesh=mesh, in_specs=in_specs, out_specs=out_specs, check_vma=False
    )
```

profile of v0, /device:TPU:1, one launch (start us, length us, event | category | flops | bytes accessed | tf_op | source)
XLA Modules:
  0.0 190.5 jit_solution(10522544885288394101)
XLA Ops:
  0.6 12.9 %gather_slots.1 = (f32[6,64,256]{2,1,0:T(8,128)}, f32[6,64,256]{2,1,0:T(8,128)}, bf16[64,120,128]{2,1,0:T(8,128)(2,1)}) custom-call(bf16[6,256,1280]{2,1,0:T(8,128)(2,1)} %tokens_ref.3, bf16[6,256,1280]{2,1,0:T(8,128)(2,1)} %grad_ref.3, bf16[64,1280]{1,0:T(8,128)(2,1)} %router_ref.3), custom_call_target="tpu_custom_call" | custom-call | tf_op jit(solution)/shard_map/gather_slots/pallas_call | solution.py:93
  13.6 38.0 %all_to_all.20.packed_ref.own_ref = bf16[64,120,128]{2,1,0:T(8,128)(2,1)} all-to-all(bf16[64,120,128]{2,1,0:T(8,128)(2,1)} %get-tuple-element.15), channel_id=1, replica_groups=mesh['exp'=64,'rep'=2] {'exp'}, dimensions={0} | all-to-all | bytes 3932160 | tf_op jit(solution)/shard_map/all_to_all | solution.py:342
  51.6 24.4 %experts.1 = (bf16[384,2560]{1,0:T(8,128)(2,1)}, bf16[384,2560]{1,0:T(8,128)(2,1)}, bf16[64,120,128]{2,1,0:T(8,128)(2,1)}) custom-call(bf16[64,120,128]{2,1,0:T(8,128)(2,1)} %all_to_all.20.packed_ref.own_ref, bf16[1,1280,2560]{2,1,0:T(8,128)(2,1)} %w_in_ref.3, bf16[1,2560,1280]{2,1,0:T(8,128)(2,1)} %w_out_ref.3), custom_call_target="tpu_custom_call" | custom-call | tf_op jit(solution)/shard_map/experts/pallas_call | solution.py:158
  76.0 0.0 copy-start
  76.0 5.9 %all-to-all-start.1 = ((bf16[64,120,128]{2,1,0:T(8,128)(2,1)}), bf16[64,120,128]{2,1,0:T(8,128)(2,1)}, u32[]{:S(2)}, u32[]{:S(2)}) async-start(bf16[64,120,128]{2,1,0:T(8,128)(2,1)} %get-tuple-element.16), calls=%async_computation.1 | async-start | bytes 3932160 | tf_op jit(solution)/shard_map/all_to_all | solution.py:342
  81.9 0.0 copy-done
  82.0 2.7 %collective-permute-start = (bf16[64,120,128]{2,1,0:T(8,128)(2,1)S(1)}, bf16[64,120,128]{2,1,0:T(8,128)(2,1)}, u32[]{:S(2)}, u32[]{:S(2)}) collective-permute-start(bf16[64,120,128]{2,1,0:T(8,128)(2,1)S(1)} %copy-done), channel_id=1, source_target_pairs={{0,1},{1,0},{2,3},{3,2},{4,5},{5,4},{6,7},{7,6},{8,9},{9,8},{10,11... | collective-permute-start | bytes 5898248 | tf_op jit(solution)/shard_map/ppermute | solution.py:351
  84.7 24.4 %all-to-all-done.1.packed_ref = bf16[64,120,128]{2,1,0:T(8,128)(2,1)} async-done(((bf16[64,120,128]{2,1,0:T(8,128)(2,1)}), bf16[64,120,128]{2,1,0:T(8,128)(2,1)}, u32[]{:S(2)}, u32[]{:S(2)}) %all-to-all-start.1) | async-done | bytes 1966112 | tf_op jit(solution)/shard_map/all_to_all | solution.py:342
  109.1 13.2 %logit_grads.1 = (bf16[6,64,256]{2,1,0:T(8,128)(2,1)}, bf16[6,64,1280]{2,1,0:T(8,128)(2,1)}, bf16[64,1280]{1,0:T(8,128)(2,1)}) custom-call(bf16[64,120,128]{2,1,0:T(8,128)(2,1)} %all-to-all-done.1.packed_ref, bf16[6,256,1280]{2,1,0:T(8,128)(2,1)} %tokens_ref.3, bf16[6,256,1280]{2,1,0:T(8,128)(2,1)} %grad_ref.3, f32[6,64,256]{2,1,0:T(8,128)} %get-tuple-element.17.disp_ref, ...), custom_call_target="tpu_custom_call" | custom-call | tf_op jit(solution)/shard_map/logit_grads/pallas_call | solution.py:227
  122.3 1.1 reshape.19
  123.4 30.5 %all_to_all.21 = bf16[128,5,128]{2,1,0:T(8,128)(2,1)S(1)} all-to-all(bf16[128,5,128]{2,1,0:T(8,128)(2,1)S(1)} %reshape.19), channel_id=1, replica_groups=mesh['exp'=64,'rep'=2] {'exp','rep'}, dimensions={0} | all-to-all | bytes 327680 | tf_op jit(solution)/shard_map/all_to_all | solution.py:342
  153.9 0.1 reduce_sum.12
  154.0 0.7 broadcast_in_dim.2
  154.8 7.3 %all-to-all-start.3 = ((bf16[128,5,128]{2,1,0:T(8,128)(2,1)}), bf16[128,5,128]{2,1,0:T(8,128)(2,1)S(1)}, u32[]{:S(2)}, u32[]{:S(2)}) async-start(bf16[128,5,128]{2,1,0:T(8,128)(2,1)} %broadcast_in_dim.2), calls=%async_computation.3 | async-start | bytes 524288 | tf_op jit(solution)/shard_map/all_to_all | solution.py:342
  162.1 6.1 %token_grads.1 = bf16[6,256,1280]{2,1,0:T(8,128)(2,1)} custom-call(bf16[6,64,256]{2,1,0:T(8,128)(2,1)} %get-tuple-element.19.lgrad_ref, f32[6,64,256]{2,1,0:T(8,128)} %get-tuple-element.17.disp_ref, bf16[6,64,1280]{2,1,0:T(8,128)(2,1)} %get-tuple-element.20.sback_ref, bf16[64,1280]{1,0:T(8,128)(2,1)} %router_ref.3), custom_call_target="tpu_custom_call" | custom-call | tf_op jit(solution)/shard_map/token_grads/pallas_call | solution.py:266
  168.2 0.0 collective-permute-done.peer_ref
  168.2 21.4 %weight_grads.1 = (bf16[1,1280,1280]{2,1,0:T(8,128)(2,1)}, bf16[1,1280,1280]{2,1,0:T(8,128)(2,1)}) custom-call(s32[1]{0:T(128)} %bitcast.start_ref, bf16[64,120,128]{2,1,0:T(8,128)(2,1)} %all_to_all.20.packed_ref.own_ref, bf16[64,120,128]{2,1,0:T(8,128)(2,1)} %collective-permute-done.peer_ref, bf16[1,1280,2560]{2,1,0:T(8,128)(2,1)} %w_in_ref.3, ...), custom_call_target="tpu_custom_call" | custom-call | tf_op jit(solution)/shard_map/weight_grads/pallas_call | solution.py:309
  189.6 0.0 all-to-all-done.3
  189.6 0.9 reshape.20
Async XLA Ops:
  76.0 5.9 %copy-start = (bf16[64,120,128]{2,1,0:T(8,128)(2,1)S(1)}, bf16[64,120,128]{2,1,0:T(8,128)(2,1)}, u32[]{:S(2)}) copy-start(bf16[64,120,128]{2,1,0:T(8,128)(2,1)} %all_to_all.20.packed_ref.own_ref) | copy-start | bytes 5898244
  76.0 33.0 %all-to-all-start.1 = ((bf16[64,120,128]{2,1,0:T(8,128)(2,1)}), bf16[64,120,128]{2,1,0:T(8,128)(2,1)}, u32[]{:S(2)}, u32[]{:S(2)}) async-start(bf16[64,120,128]{2,1,0:T(8,128)(2,1)} %get-tuple-element.16), calls=%async_computation.1 | async-start | bytes 3932160 | tf_op jit(solution)/shard_map/all_to_all | solution.py:342
  82.0 86.2 %collective-permute-start = (bf16[64,120,128]{2,1,0:T(8,128)(2,1)S(1)}, bf16[64,120,128]{2,1,0:T(8,128)(2,1)}, u32[]{:S(2)}, u32[]{:S(2)}) collective-permute-start(bf16[64,120,128]{2,1,0:T(8,128)(2,1)S(1)} %copy-done), channel_id=1, source_target_pairs={{0,1},{1,0},{2,3},{3,2},{4,5},{5,4},{6,7},{7,6},{8,9},{9,8},{10,11... | collective-permute-start | bytes 5898248 | tf_op jit(solution)/shard_map/ppermute | solution.py:351
  154.8 34.8 %all-to-all-start.3 = ((bf16[128,5,128]{2,1,0:T(8,128)(2,1)}), bf16[128,5,128]{2,1,0:T(8,128)(2,1)S(1)}, u32[]{:S(2)}, u32[]{:S(2)}) async-start(bf16[128,5,128]{2,1,0:T(8,128)(2,1)} %broadcast_in_dim.2), calls=%async_computation.3 | async-start | bytes 524288 | tf_op jit(solution)/shard_map/all_to_all | solution.py:342
where the time goes:
time: 191 us; the launch traced here: 190 us
  Pallas kernels  78.1 us (41%)
  blocking collectives  68.5 us (36%)
  waiting for transfers between devices  24.4 us (13%)
  starting transfers between devices  15.9 us (8%)
  local copies, waits for them, and re-layouts  2.77 us (1%)
    all_to_all x2, blocking collectives, swap(): return lax.all_to_all(value, axis, split_axis=0, concat_axis=0, tiled=True)  68.5 us
    pallas_call x1, Pallas kernels, experts(): pl.pallas_call(functools.partial(expert_body, rows // groups), grid=(hidd...  24.4 us
    all_to_all x2, waiting for transfers between devices, swap(): return lax.all_to_all(value, axis, split_axis=0, concat_axis=0, tiled=True)  24.4 us
    pallas_call x1, Pallas kernels, weight_grads(): pl.pallas_call(functools.partial(weight_body, rows // groups), grid_spec=...  21.4 us
    pallas_call x1, Pallas kernels, logit_grads(): pl.pallas_call(functools.partial(logit_body, images), grid=(images,), in_...  13.2 us
    all_to_all x2, starting transfers between devices, swap(): return lax.all_to_all(value, axis, split_axis=0, concat_axis=0, tiled=True)  13.2 us
    pallas_call x1, Pallas kernels, gather_slots(): pl.pallas_call(functools.partial(gather_body, images), grid=(images,), in...  12.9 us
    pallas_call x1, Pallas kernels, token_grads(): pl.pallas_call(token_body, grid=(images,), in_specs=[pl.BlockSpec((1, slo...  6.07 us
  transfers between devices with their start and end apart: 3, of which 1 were waited for; matrix products, arithmetic and copies ran while one was open for 1% of the time, Pallas kernels for 21%

commit v1 on v0

v1 whole, which is shorter than its diff:
```python
import functools

import jax
import jax.numpy as jnp
from jax import lax
from jax.experimental import pallas as pl
from jax.experimental.pallas import tpu as pltpu
from jax.sharding import PartitionSpec as P

BF16, F32 = jnp.bfloat16, jnp.float32
NN, NT, TN = ((1,), (0,)), ((1,), (1,)), ((0,), (0,))
VMEM_LIMIT = 56 * 2**20
LANES = 128
SUBLANES = 8
PITCH_PAD = 8


def mm(a, b, dims):
    return lax.dot_general(a, b, (dims, ((), ())), preferred_element_type=F32)


def params():
    return pltpu.CompilerParams(vmem_limit_bytes=VMEM_LIMIT)


def gelu_parts(hidden):
    cdf = 0.5 * (1.0 + lax.erf(hidden * 0.7071067811865476))
    density = jnp.exp(-0.5 * hidden * hidden) * 0.3989422804014327
    return hidden * cdf, cdf + hidden * density


def pitch_of(groups):
    return groups + PITCH_PAD


def stage_rows(packed_refs, stage_ref):
    rows = packed_refs[0].shape[1]
    pitch = stage_ref.shape[0] // rows
    first = 0
    for packed_ref in packed_refs:
        groups = packed_ref.shape[0]

        def body(g, carry, packed_ref=packed_ref, first=first):
            stage_ref[pl.ds(first + g, rows, stride=pitch), :] = packed_ref[g].astype(F32)
            return carry

        lax.fori_loop(0, groups, body, 0, unroll=8)
        first += groups


def pack_rows(stage_ref, packed_ref):
    groups, rows, _ = packed_ref.shape

    def body(g, carry):
        packed_ref[g] = stage_ref[pl.ds(g, rows, stride=pitch_of(groups)), :].astype(BF16)
        return carry

    lax.fori_loop(0, groups, body, 0, unroll=8)


def piece_rows(piece, which, image, images, groups):
    start = ((piece * 2 + which) * images + image) * pitch_of(groups)
    return pl.ds(start if isinstance(start, int) else pl.multiple_of(start, 8), groups)


def image_rows(stage_ref, which, image, images, groups):
    pieces = stage_ref.shape[0] // (2 * images * pitch_of(groups))
    parts = [stage_ref[piece_rows(p, which, image, images, groups), :] for p in range(pieces)]
    return jnp.concatenate([part.astype(BF16) for part in parts], axis=1)


def put_image(stage_ref, value, which, image, images, groups):
    for p in range(value.shape[1] // LANES):
        cols = value[:, p * LANES : (p + 1) * LANES]
        stage_ref[piece_rows(p, which, image, images, groups), :] = cols


def load_rows(stage_ref, row_ref, first, which, images, groups):
    for image in range(images):
        where = slice(first + image * groups, first + (image + 1) * groups)
        row_ref[where, :] = image_rows(stage_ref, which, image, images, groups)


def stage_shape(packed_shape):
    return pltpu.VMEM((pitch_of(packed_shape[0]) * packed_shape[1], LANES), F32)


def gather_body(images, tokens_ref, grad_ref, router_ref, disp_ref, comb_ref, packed_ref, stage_ref):
    i = pl.program_id(0)
    slots = router_ref.shape[0]
    each = tokens_ref.shape[0]
    for j in range(each):
        tok = tokens_ref[j]
        logits = mm(router_ref[...], tok, NT)
        d_exp = jnp.exp(logits - jnp.max(logits, axis=1, keepdims=True))
        dispatch = d_exp / jnp.sum(d_exp, axis=1, keepdims=True)
        c_exp = jnp.exp(logits - jnp.max(logits, axis=0, keepdims=True))
        combine = c_exp / jnp.sum(c_exp, axis=0, keepdims=True)
        disp_ref[j] = dispatch
        comb_ref[j] = combine
        slot_in = mm(dispatch.astype(BF16), tok, NN)
        slot_grad = mm(combine.astype(BF16), grad_ref[j], NN)
        put_image(stage_ref, slot_in, 0, i * each + j, images, slots)
        put_image(stage_ref, slot_grad, 1, i * each + j, images, slots)

    @pl.when(i == pl.num_programs(0) - 1)
    def _():
        pack_rows(stage_ref, packed_ref)


def gather_slots(tokens, out_grad, router, each):
    images, toks, width = tokens.shape
    slots = router.shape[0]
    packed = (slots, 2 * images * width // LANES, LANES)
    image = lambda i: (i, 0, 0)
    return pl.pallas_call(
        functools.partial(gather_body, images),
        grid=(images // each,),
        in_specs=[
            pl.BlockSpec((each, toks, width), image),
            pl.BlockSpec((each, toks, width), image),
            pl.BlockSpec((slots, width), lambda i: (0, 0)),
        ],
        out_specs=[
            pl.BlockSpec((each, slots, toks), image),
            pl.BlockSpec((each, slots, toks), image),
            pl.BlockSpec(packed, lambda i: (0, 0, 0)),
        ],
        out_shape=[
            jax.ShapeDtypeStruct((images, slots, toks), F32),
            jax.ShapeDtypeStruct((images, slots, toks), F32),
            jax.ShapeDtypeStruct(packed, BF16),
        ],
        scratch_shapes=[stage_shape(packed)],
        compiler_params=params(),
        name="gather_slots",
    )(tokens, out_grad, router)


def expert_body(images, packed_ref, w_in_ref, w_out_ref, act_ref, dhid_ref, back_ref, in_ref, grad_ref,
                stage_ref, out_acc, back_acc):
    f = pl.program_id(0)
    groups = packed_ref.shape[0]

    @pl.when(f == 0)
    def _():
        stage_rows((packed_ref,), stage_ref)
        load_rows(stage_ref, in_ref, 0, 0, images, groups)
        load_rows(stage_ref, grad_ref, 0, 1, images, groups)
        out_acc[...] = jnp.zeros_like(out_acc)
        back_acc[...] = jnp.zeros_like(back_acc)

    w_in, w_out = w_in_ref[0], w_out_ref[0]
    act, slope = gelu_parts(mm(in_ref[...], w_in, NN))
    act = act.astype(BF16)
    act_ref[...] = act
    dhid = (mm(grad_ref[...], w_out, NT) * slope).astype(BF16)
    dhid_ref[...] = dhid
    out_acc[...] += mm(act, w_out, NN)
    back_acc[...] += mm(dhid, w_in, NT)

    @pl.when(f == pl.num_programs(0) - 1)
    def _():
        for image in range(images):
            where = slice(image * groups, (image + 1) * groups)
            put_image(stage_ref, out_acc[where, :], 0, image, images, groups)
            put_image(stage_ref, back_acc[where, :], 1, image, images, groups)
        pack_rows(stage_ref, back_ref)


def experts(packed, w_in, w_out, block):
    width, hidden = w_in.shape[1:]
    groups = packed.shape[0]
    rows = packed.shape[1] * LANES // (2 * width) * groups
    return pl.pallas_call(
        functools.partial(expert_body, rows // groups),
        grid=(hidden // block,),
        in_specs=[
            pl.BlockSpec(packed.shape, lambda f: (0, 0, 0)),
            pl.BlockSpec((1, width, block), lambda f: (0, 0, f)),
            pl.BlockSpec((1, block, width), lambda f: (0, f, 0)),
        ],
        out_specs=[
            pl.BlockSpec((rows, block), lambda f: (0, f)),
            pl.BlockSpec((rows, block), lambda f: (0, f)),
            pl.BlockSpec(packed.shape, lambda f: (0, 0, 0)),
            pl.BlockSpec((rows, width), lambda f: (0, 0)),
            pl.BlockSpec((rows, width), lambda f: (0, 0)),
        ],
        out_shape=[
            jax.ShapeDtypeStruct((rows, hidden), BF16),
            jax.ShapeDtypeStruct((rows, hidden), BF16),
            jax.ShapeDtypeStruct(packed.shape, BF16),
            jax.ShapeDtypeStruct((rows, width), BF16),
            jax.ShapeDtypeStruct((rows, width), BF16),
        ],
        scratch_shapes=[
            stage_shape(packed.shape),
            pltpu.VMEM((rows, width), F32),
            pltpu.VMEM((rows, width), F32),
        ],
        compiler_params=params(),
        name="experts",
    )(packed, w_in, w_out)


def logit_body(images, packed_ref, tokens_ref, grad_ref, disp_ref, comb_ref, lgrad_ref, sback_ref, router_ref,
               stage_ref, acc_ref):
    i = pl.program_id(0)
    slots = packed_ref.shape[0]

    @pl.when(i == 0)
    def _():
        stage_rows((packed_ref,), stage_ref)
        acc_ref[...] = jnp.zeros_like(acc_ref)

    each = tokens_ref.shape[0]
    for j in range(each):
        slot_out = image_rows(stage_ref, 0, i * each + j, images, slots)
        slot_back = image_rows(stage_ref, 1, i * each + j, images, slots)
        sback_ref[j] = slot_back
        tok = tokens_ref[j]
        comb_dot = mm(slot_out, grad_ref[j], NT)
        disp_dot = mm(slot_back, tok, NT)
        combine, dispatch = comb_ref[j], disp_ref[j]
        comb_part = combine * (comb_dot - jnp.sum(combine * comb_dot, axis=0, keepdims=True))
        disp_part = dispatch * (disp_dot - jnp.sum(dispatch * disp_dot, axis=1, keepdims=True))
        lgrad = (comb_part + disp_part).astype(BF16)
        lgrad_ref[j] = lgrad
        acc_ref[...] += mm(lgrad, tok, NN)

    @pl.when(i == pl.num_programs(0) - 1)
    def _():
        tiles = 0
        for first in range(0, slots, SUBLANES):
            for col in range(0, acc_ref.shape[1], LANES):
                tile = acc_ref[first : first + SUBLANES, col : col + LANES]
                router_ref[tiles] = tile.astype(BF16)
                tiles += 1
        router_ref[tiles:] = jnp.zeros((router_ref.shape[0] - tiles, SUBLANES, LANES), BF16)


def logit_grads(packed, tokens, out_grad, dispatch, combine, devices, each):
    images, toks, width = tokens.shape
    slots = packed.shape[0]
    assert slots * width <= devices * SUBLANES * LANES
    image = lambda i: (i, 0, 0)
    return pl.pallas_call(
        functools.partial(logit_body, images),
        grid=(images // each,),
        in_specs=[
            pl.BlockSpec(packed.shape, lambda i: (0, 0, 0)),
            pl.BlockSpec((each, toks, width), image),
            pl.BlockSpec((each, toks, width), image),
            pl.BlockSpec((each, slots, toks), image),
            pl.BlockSpec((each, slots, toks), image),
        ],
        out_specs=[
            pl.BlockSpec((each, slots, toks), image),
            pl.BlockSpec((each, slots, width), image),
            pl.BlockSpec((devices, SUBLANES, LANES), lambda i: (0, 0, 0)),
        ],
        out_shape=[
            jax.ShapeDtypeStruct((images, slots, toks), BF16),
            jax.ShapeDtypeStruct((images, slots, width), BF16),
            jax.ShapeDtypeStruct((devices, SUBLANES, LANES), BF16),
        ],
        scratch_shapes=[
            stage_shape(packed.shape),
            pltpu.VMEM((slots, width), F32),
        ],
        compiler_params=params(),
        name="logit_grads",
    )(packed, tokens, out_grad, dispatch, combine)


def token_body(lgrad_ref, disp_ref, sback_ref, router_ref, out_ref):
    for j in range(out_ref.shape[0]):
        left = jnp.concatenate([lgrad_ref[j], disp_ref[j].astype(BF16)], axis=0)
        right = jnp.concatenate([router_ref[...], sback_ref[j]], axis=0)
        out_ref[j] = mm(left, right, TN).astype(BF16)


def token_grads(lgrad, dispatch, slot_back, router, each):
    images, slots, toks = lgrad.shape
    width = router.shape[1]
    image = lambda i: (i, 0, 0)
    return pl.pallas_call(
        token_body,
        grid=(images // each,),
        in_specs=[
            pl.BlockSpec((each, slots, toks), image),
            pl.BlockSpec((each, slots, toks), image),
            pl.BlockSpec((each, slots, width), image),
            pl.BlockSpec((slots, width), lambda i: (0, 0)),
        ],
        out_specs=pl.BlockSpec((each, toks, width), image),
        out_shape=jax.ShapeDtypeStruct((images, toks, width), BF16),
        compiler_params=params(),
        name="token_grads",
    )(lgrad, dispatch, slot_back, router)


def weight_body(images, n_packed, n_own, n_first, start_ref, *refs):
    del start_ref
    packed_refs, refs = refs[:n_packed], refs[n_packed:]
    (w_in_ref, w_out_ref), refs = refs[:2], refs[2:]
    own_refs, refs = refs[:n_own], refs[n_own:]
    first_refs, refs = refs[:n_first], refs[n_first:]
    gin_ref, gout_ref, stage_ref, in_ref, grad_ref = refs
    groups = sum(packed_ref.shape[0] for packed_ref in packed_refs)

    @pl.when(pl.program_id(0) == 0)
    def _():
        stage_rows(packed_refs, stage_ref)
        load_rows(stage_ref, in_ref, 0, 0, images, groups)
        load_rows(stage_ref, grad_ref, 0, 1, images, groups)

    act, slope = gelu_parts(mm(in_ref[...], w_in_ref[0], NN))
    dhid = (mm(grad_ref[...], w_out_ref[0], NT) * slope).astype(BF16)
    gin = mm(in_ref[...], dhid, TN)
    gout = mm(act.astype(BF16), grad_ref[...], TN)
    if n_own:
        own_in_ref, own_grad_ref, own_act_ref, own_dhid_ref = own_refs
        gin += mm(own_in_ref[...], own_dhid_ref[...], TN)
        gout += mm(own_act_ref[...], own_grad_ref[...], TN)
    if n_first:
        gin += first_refs[0][0].astype(F32)
        gout += first_refs[1][0].astype(F32)
    gin_ref[0] = gin.astype(gin_ref.dtype)
    gout_ref[0] = gout.astype(gout_ref.dtype)


def weight_grads(start, packed, w_in, w_out, own, first, block, reps, dtype, name):
    width, hidden = w_in.shape[1], w_in.shape[2] // reps
    groups, pieces = sum(p.shape[0] for p in packed), packed[0].shape[1]
    images = pieces * LANES // (2 * width)
    rows = images * groups
    in_specs = [pl.BlockSpec(v.shape, lambda f, s: (0, 0, 0)) for v in packed]
    in_specs += [
        pl.BlockSpec((1, width, block), lambda f, s: (0, 0, s[0] + f)),
        pl.BlockSpec((1, block, width), lambda f, s: (0, s[0] + f, 0)),
    ]
    if own:
        own_rows = own[0].shape[0]
        in_specs += [pl.BlockSpec((own_rows, width), lambda f, s: (0, 0))] * 2
        in_specs += [pl.BlockSpec((own_rows, block), lambda f, s: (0, s[0] + f))] * 2
    outs = [
        pl.BlockSpec((1, width, block), lambda f, s: (0, 0, f)),
        pl.BlockSpec((1, block, width), lambda f, s: (0, f, 0)),
    ]
    if first:
        in_specs += outs
    return pl.pallas_call(
        functools.partial(weight_body, images, len(packed), len(own), len(first)),
        grid_spec=pltpu.PrefetchScalarGridSpec(
            num_scalar_prefetch=1,
            grid=(hidden // block,),
            in_specs=in_specs,
            out_specs=outs,
            scratch_shapes=[
                stage_shape((groups, pieces)),
                pltpu.VMEM((rows, width), BF16),
                pltpu.VMEM((rows, width), BF16),
            ],
        ),
        out_shape=[
            jax.ShapeDtypeStruct((1, width, hidden), dtype),
            jax.ShapeDtypeStruct((1, hidden, width), dtype),
        ],
        compiler_params=params(),
        name=name,
    )(start, *packed, w_in, w_out, *own, *first)


def swap(value, axis):
    return lax.all_to_all(value, axis, split_axis=0, concat_axis=0, tiled=True)


def per_device(tokens, out_grad, router, w_in, w_out):
    reps = lax.axis_size("rep")
    devices = lax.axis_size("exp") * reps
    slots, width = router.shape
    dispatch, combine, to_experts = gather_slots(tokens, out_grad, router, 3)
    own = swap(to_experts, "exp")
    act, dhid, to_images, row_in, row_grad = experts(own, w_in, w_out, 512)
    hidden, block = w_in.shape[2] // reps, 640
    start = (lax.axis_index("rep") * (hidden // block)).astype(jnp.int32).reshape(1)
    pairs = [(i, i ^ 1) for i in range(reps)]
    cut = own.shape[0] * 3 // 8
    peer_first = lax.ppermute(own[:cut], "rep", pairs)
    peer_last = lax.ppermute(own[cut:], "rep", pairs)
    to_images, peer_first = lax.optimization_barrier((to_images, peer_first))
    back = swap(to_images, "exp")
    own_rows = (row_in, row_grad, act, dhid)
    first = weight_grads(start, [peer_first], w_in, w_out, own_rows, (), block, reps, F32, "weight_first")
    back, first = lax.optimization_barrier((back, first))
    lgrad, slot_back, tiles = logit_grads(back, tokens, out_grad, dispatch, combine, devices, 2)
    start, tiles = lax.optimization_barrier((start, tiles))
    shares = swap(tiles, ("exp", "rep")).astype(F32)
    share = jnp.sum(shares, axis=0).astype(BF16)
    token_grad = token_grads(lgrad, dispatch, slot_back, router, 3)
    share, token_grad = lax.optimization_barrier((share, token_grad))
    start, share = lax.optimization_barrier((start, share))
    tiles = swap(jnp.broadcast_to(share[None], shares.shape), ("exp", "rep"))
    tiles = tiles[: slots * width // (SUBLANES * LANES)].reshape(slots // SUBLANES, width // LANES, SUBLANES, LANES)
    router_grad = tiles.transpose(0, 2, 1, 3).reshape(slots, width).astype(F32)
    grad_in, grad_out = weight_grads(start, [peer_last], w_in, w_out, (), first, block, reps, BF16, "weight_last")
    return token_grad, grad_in, grad_out, router_grad


def solution(mesh):
    in_specs = (
        P(("exp", "rep"), None, None),
        P(("exp", "rep"), None, None),
        P(),
        P("exp", None, None),
        P("exp", None, None),
    )
    out_specs = (P(("exp", "rep"), None, None), P("exp", None, "rep"), P("exp", "rep", None), P())
    return jax.shard_map(
        per_device, mesh=mesh, in_specs=in_specs, out_specs=out_specs, check_vma=False
    )
```

time: 191 us -> 152 us (0.80)
  blocking collectives: 68.5 us -> 37.9 us
  Pallas kernels: 78.1 us -> 65.3 us
  starting transfers between devices: 15.9 us -> 23.9 us
  waiting for transfers between devices: 24.4 us -> 20.6 us
    all_to_all x2 -> x1, blocking collectives: 68.5 us -> 37.9 us  [swap(): return lax.all_to_all(value, axis, split_axis=0, concat_axis=0, tiled=True)]
    all_to_all x2 -> x3, starting transfers between devices: 13.2 us -> 19.9 us  [swap(): return lax.all_to_all(value, axis, split_axis=0, concat_axis=0, tiled=True)]
    pallas_call x4 -> x5, Pallas kernels: 53.6 us -> 47.1 us  [the longest x2 25.8 us: weight_grads(): pl.pallas_call(functools.partial(weight_body, images, len(packed), len(ow...]
    pallas_call x1, Pallas kernels: 24.4 us -> 18.1 us  [experts(): pl.pallas_call(functools.partial(expert_body, rows // groups), grid=(hidd...]
    all_to_all x2 -> x3, waiting for transfers between devices: 24.4 us -> 20.6 us  [swap(): return lax.all_to_all(value, axis, split_axis=0, concat_axis=0, tiled=True)]
    ppermute x1 -> x2, starting transfers between devices: 2.7 us -> 3.97 us  [the longest x1 2.7 us: per_device(): peer_first = lax.ppermute(own[:cut], 'rep', pairs)]
  transfers between devices with their start and end apart: 3 -> 5, of which waited for: 1 -> 2; matrix products, arithmetic and copies ran while one was open for 1% -> 1% of each run, Pallas kernels for 21% -> 38%
where the time goes in v1:
time: 152 us; the launch traced here: 151 us
  Pallas kernels  65.3 us (43%)
  blocking collectives  37.9 us (25%)
  starting transfers between devices  23.9 us (16%)
  waiting for transfers between devices  20.6 us (14%)
  local copies, waits for them, and re-layouts  1.93 us (1%)
    all_to_all x1, blocking collectives, swap(): return lax.all_to_all(value, axis, split_axis=0, concat_axis=0, tiled=True)  37.9 us
    pallas_call x2, Pallas kernels, weight_grads(): pl.pallas_call(functools.partial(weight_body, images, len(packed), len(ow...  25.8 us
    all_to_all x3, waiting for transfers between devices, swap(): return lax.all_to_all(value, axis, split_axis=0, concat_axis=0, tiled=True)  20.6 us
    all_to_all x3, starting transfers between devices, swap(): return lax.all_to_all(value, axis, split_axis=0, concat_axis=0, tiled=True)  19.9 us
    pallas_call x1, Pallas kernels, experts(): pl.pallas_call(functools.partial(expert_body, rows // groups), grid=(hidd...  18.1 us
    pallas_call x1, Pallas kernels, logit_grads(): pl.pallas_call(functools.partial(logit_body, images), grid=(images // eac...  9.4 us
    pallas_call x1, Pallas kernels, gather_slots(): pl.pallas_call(functools.partial(gather_body, images), grid=(images // ea...  7.9 us
    pallas_call x1, Pallas kernels, token_grads(): pl.pallas_call(token_body, grid=(images // each,), in_specs=[pl.BlockSpec...  4 us
  transfers between devices with their start and end apart: 5, of which 2 were waited for; matrix products, arithmetic and copies ran while one was open for 1% of the time, Pallas kernels for 38%

profile of v1, /device:TPU:1, one launch (start us, length us, event | category | flops | bytes accessed | tf_op | source)
XLA Modules:
  0.0 151.2 jit_solution(13807637352456490134)
XLA Ops:
  0.6 7.9 %gather_slots.1 = (f32[6,64,256]{2,1,0:T(8,128)}, f32[6,64,256]{2,1,0:T(8,128)}, bf16[64,120,128]{2,1,0:T(8,128)(2,1)}) custom-call(bf16[6,256,1280]{2,1,0:T(8,128)(2,1)} %tokens_ref.3, bf16[6,256,1280]{2,1,0:T(8,128)(2,1)} %grad_ref.3, bf16[64,1280]{1,0:T(8,128)(2,1)} %router_ref.3), custom_call_target="tpu_custom_call" | custom-call | tf_op jit(solution)/shard_map/gather_slots/pallas_call | solution.py:116
  8.5 37.9 %all_to_all.20.packed_ref = bf16[64,120,128]{2,1,0:T(8,128)(2,1)S(1)} all-to-all(bf16[64,120,128]{2,1,0:T(8,128)(2,1)} %get-tuple-element.30), channel_id=1, replica_groups=mesh['exp'=64,'rep'=2] {'exp'}, dimensions={0} | all-to-all | bytes 3932160 | tf_op jit(solution)/shard_map/all_to_all | solution.py:377
  46.4 0.0 copy-start
  46.4 0.1 slice.12
  46.5 2.7 %collective-permute-start = (bf16[24,120,128]{2,1,0:T(8,128)(2,1)S(1)}, bf16[24,120,128]{2,1,0:T(8,128)(2,1)}, u32[]{:S(2)}, u32[]{:S(2)}) collective-permute-start(bf16[24,120,128]{2,1,0:T(8,128)(2,1)S(1)} %slice.12), channel_id=1, source_target_pairs={{0,1},{1,0},{2,3},{3,2},{4,5},{5,4},{6,7},{7,6},{8,9},{9,8},{10,11... | collective-permute-start | bytes 2211848 | tf_op jit(solution)/shard_map/ppermute | solution.py:391
  49.2 0.0 copy-done
  49.2 18.1 %experts.1 = (bf16[384,2560]{1,0:T(8,128)(2,1)}, bf16[384,2560]{1,0:T(8,128)(2,1)}, bf16[64,120,128]{2,1,0:T(8,128)(2,1)}, bf16[384,1280]{1,0:T(8,128)(2,1)}, bf16[384,1280]{1,0:T(8,128)(2,1)}) custom-call(bf16[64,120,128]{2,1,0:T(8,128)(2,1)} %copy-done, bf16[1,1280,2560]{2,1,0:T(8,128)(2,1)} %refs_1_.3, bf16[1,2560,1280]{2,1,0:T(8,128)(2,1)} %refs_2_.3), custom_call_target="tpu_custom_call" | custom-call | tf_op jit(solution)/shard_map/experts/pallas_call | solution.py:175
  67.3 0.0 copy-start.1
  67.3 0.0 collective-permute-done.refs_0_
  67.3 6.2 %all-to-all-start.1 = ((bf16[64,120,128]{2,1,0:T(8,128)(2,1)}), bf16[64,120,128]{2,1,0:T(8,128)(2,1)}, u32[]{:S(2)}, u32[]{:S(2)}) async-start(bf16[64,120,128]{2,1,0:T(8,128)(2,1)} %get-tuple-element.32), calls=%async_computation.1 | async-start | bytes 3932160 | tf_op jit(solution)/shard_map/all_to_all | solution.py:377
  73.6 0.0 copy-done.1
  73.6 0.1 slice.13
  73.7 1.3 collective-permute-start.1
  74.9 14.2 %weight_first.1 = (f32[1,1280,1280]{2,1,0:T(8,128)}, f32[1,1280,1280]{2,1,0:T(8,128)}) custom-call(s32[1]{0:T(128)} %bitcast.start_ref, bf16[24,120,128]{2,1,0:T(8,128)(2,1)} %collective-permute-done.refs_0_, bf16[1,1280,2560]{2,1,0:T(8,128)(2,1)} %refs_1_.3, bf16[1,2560,1280]{2,1,0:T(8,128)(2,1)} %refs_2_.3, bf16[384,1280]{1,0:T(8,128)(2,1)} %get-tuple-element.34.refs_3_, ...), custom_call_target="tpu_custom_call" | custom-call | tf_op jit(solution)/shard_map/weight_first/pallas_call | solution.py:354
  89.1 11.5 %all-to-all-done.1.packed_ref = bf16[64,120,128]{2,1,0:T(8,128)(2,1)} async-done(((bf16[64,120,128]{2,1,0:T(8,128)(2,1)}), bf16[64,120,128]{2,1,0:T(8,128)(2,1)}, u32[]{:S(2)}, u32[]{:S(2)}) %all-to-all-start.1) | async-done | bytes 1966112 | tf_op jit(solution)/shard_map/all_to_all | solution.py:377
  100.7 9.4 %logit_grads.1 = (bf16[6,64,256]{2,1,0:T(8,128)(2,1)}, bf16[6,64,1280]{2,1,0:T(8,128)(2,1)}, bf16[128,8,128]{2,1,0:T(8,128)(2,1)}) custom-call(bf16[64,120,128]{2,1,0:T(8,128)(2,1)} %all-to-all-done.1.packed_ref, bf16[6,256,1280]{2,1,0:T(8,128)(2,1)} %tokens_ref.3, bf16[6,256,1280]{2,1,0:T(8,128)(2,1)} %grad_ref.3, ...), custom_call_target="tpu_custom_call" | custom-call | tf_op jit(solution)/shard_map/logit_grads/pallas_call | solution.py:248
  110.1 5.4 %all-to-all-start.2 = ((bf16[128,8,128]{2,1,0:T(8,128)(2,1)}), bf16[128,8,128]{2,1,0:T(8,128)(2,1)S(1)}, u32[]{:S(2)}, u32[]{:S(2)}) async-start(bf16[128,8,128]{2,1,0:T(8,128)(2,1)} %get-tuple-element.44), calls=%async_computation.2 | async-start | bytes 524288 | tf_op jit(solution)/shard_map/all_to_all | solution.py:377
  115.5 4.0 %token_grads.1 = bf16[6,256,1280]{2,1,0:T(8,128)(2,1)} custom-call(bf16[6,64,256]{2,1,0:T(8,128)(2,1)} %get-tuple-element.45.lgrad_ref, f32[6,64,256]{2,1,0:T(8,128)} %get-tuple-element.41.disp_ref, bf16[6,64,1280]{2,1,0:T(8,128)(2,1)} %get-tuple-element.46.sback_ref, bf16[64,1280]{1,0:T(8,128)(2,1)} %router_ref.3), custom_call_target="tpu_custom_call" | custom-call | tf_op jit(solution)/shard_map/token_grads/pallas_call | solution.py:288
  119.5 9.1 %all-to-all-done.2 = bf16[128,8,128]{2,1,0:T(8,128)(2,1)S(1)} async-done(((bf16[128,8,128]{2,1,0:T(8,128)(2,1)}), bf16[128,8,128]{2,1,0:T(8,128)(2,1)S(1)}, u32[]{:S(2)}, u32[]{:S(2)}) %all-to-all-start.2) | async-done | bytes 262176 | tf_op jit(solution)/shard_map/all_to_all | solution.py:377
  128.5 0.1 reduce_sum.12
  128.7 0.7 broadcast_in_dim.2
  129.4 8.3 %all-to-all-start.3 = ((bf16[128,8,128]{2,1,0:T(8,128)(2,1)}), bf16[128,8,128]{2,1,0:T(8,128)(2,1)S(1)}, u32[]{:S(2)}, u32[]{:S(2)}) async-start(bf16[128,8,128]{2,1,0:T(8,128)(2,1)} %broadcast_in_dim.2), calls=%async_computation.3 | async-start | bytes 524288 | tf_op jit(solution)/shard_map/all_to_all | solution.py:377
  137.7 0.0 collective-permute-done.1.refs_0_
  137.7 0.0 copy-start.2
  137.7 1.0 copy-done.2
  138.8 11.6 %weight_last.1 = (bf16[1,1280,1280]{2,1,0:T(8,128)(2,1)}, bf16[1,1280,1280]{2,1,0:T(8,128)(2,1)}) custom-call(s32[1]{0:T(128)} %bitcast.start_ref, bf16[40,120,128]{2,1,0:T(8,128)(2,1)} %copy-done.2, bf16[1,1280,2560]{2,1,0:T(8,128)(2,1)} %refs_1_.3, bf16[1,2560,1280]{2,1,0:T(8,128)(2,1)} %refs_2_.3, f32[1,1280,1280]{2,1,0:T(8,128)} %get-tuple-element.51.refs_3_, ...), custom_call_target="tpu_custom_call" | custom-call | tf_op jit(solution)/shard_map/weight_last/pallas_call | solution.py:354
  150.4 0.0 all-to-all-done.3
  150.4 0.7 convert_bitcast_fusion
  (1 shorter events, 0.0 us)
Async XLA Ops:
  46.4 2.8 %copy-start = (bf16[64,120,128]{2,1,0:T(8,128)(2,1)}, bf16[64,120,128]{2,1,0:T(8,128)(2,1)S(1)}, u32[]{:S(2)}) copy-start(bf16[64,120,128]{2,1,0:T(8,128)(2,1)S(1)} %all_to_all.20.packed_ref) | copy-start | bytes 5898244
  46.5 20.8 %collective-permute-start = (bf16[24,120,128]{2,1,0:T(8,128)(2,1)S(1)}, bf16[24,120,128]{2,1,0:T(8,128)(2,1)}, u32[]{:S(2)}, u32[]{:S(2)}) collective-permute-start(bf16[24,120,128]{2,1,0:T(8,128)(2,1)S(1)} %slice.12), channel_id=1, source_target_pairs={{0,1},{1,0},{2,3},{3,2},{4,5},{5,4},{6,7},{7,6},{8,9},{9,8},{10,11... | collective-permute-start | bytes 2211848 | tf_op jit(solution)/shard_map/ppermute | solution.py:391
  67.3 6.2 %copy-start.1 = (bf16[64,120,128]{2,1,0:T(8,128)(2,1)S(1)}, bf16[64,120,128]{2,1,0:T(8,128)(2,1)}, u32[]{:S(2)}) copy-start(bf16[64,120,128]{2,1,0:T(8,128)(2,1)} %copy-done) | copy-start | bytes 5898244
  67.3 33.3 %all-to-all-start.1 = ((bf16[64,120,128]{2,1,0:T(8,128)(2,1)}), bf16[64,120,128]{2,1,0:T(8,128)(2,1)}, u32[]{:S(2)}, u32[]{:S(2)}) async-start(bf16[64,120,128]{2,1,0:T(8,128)(2,1)} %get-tuple-element.32), calls=%async_computation.1 | async-start | bytes 3932160 | tf_op jit(solution)/shard_map/all_to_all | solution.py:377
  73.7 64.1 %collective-permute-start.1 = (bf16[40,120,128]{2,1,0:T(8,128)(2,1)S(1)}, bf16[40,120,128]{2,1,0:T(8,128)(2,1)S(1)}, u32[]{:S(2)}, u32[]{:S(2)}) collective-permute-start(bf16[40,120,128]{2,1,0:T(8,128)(2,1)S(1)} %slice.13), channel_id=1, source_target_pairs={{0,1},{1,0},{2,3},{3,2},{4,5},{5,4},{6,7},{7,6},{8,9},{9,8},{10,11... | collective-permute-start | bytes 3686408 | tf_op jit(solution)/shard_map/ppermute | solution.py:392
  110.1 18.5 %all-to-all-start.2 = ((bf16[128,8,128]{2,1,0:T(8,128)(2,1)}), bf16[128,8,128]{2,1,0:T(8,128)(2,1)S(1)}, u32[]{:S(2)}, u32[]{:S(2)}) async-start(bf16[128,8,128]{2,1,0:T(8,128)(2,1)} %get-tuple-element.44), calls=%async_computation.2 | async-start | bytes 524288 | tf_op jit(solution)/shard_map/all_to_all | solution.py:377
  129.4 21.0 %all-to-all-start.3 = ((bf16[128,8,128]{2,1,0:T(8,128)(2,1)}), bf16[128,8,128]{2,1,0:T(8,128)(2,1)S(1)}, u32[]{:S(2)}, u32[]{:S(2)}) async-start(bf16[128,8,128]{2,1,0:T(8,128)(2,1)} %broadcast_in_dim.2), calls=%async_computation.3 | async-start | bytes 524288 | tf_op jit(solution)/shard_map/all_to_all | solution.py:377
  137.7 1.0 copy-start.2

commit v2 on v1

--- a/solution.py
+++ b/solution.py
@@ -19,8 +19,8 @@
     return lax.dot_general(a, b, (dims, ((), ())), preferred_element_type=F32)
 
 
-def params():
-    return pltpu.CompilerParams(vmem_limit_bytes=VMEM_LIMIT)
+def params(limit=VMEM_LIMIT):
+    return pltpu.CompilerParams(vmem_limit_bytes=limit)
 
 
 def gelu_parts(hidden):
@@ -82,7 +82,7 @@
 
 
 def stage_shape(packed_shape):
-    return pltpu.VMEM((pitch_of(packed_shape[0]) * packed_shape[1], LANES), F32)
+    return pltpu.VMEM((pitch_of(packed_shape[0]) * (packed_shape[1] + 1), LANES), F32)
 
 
 def gather_body(images, tokens_ref, grad_ref, router_ref, disp_ref, comb_ref, packed_ref, stage_ref):
@@ -137,8 +137,8 @@
     )(tokens, out_grad, router)
 
 
-def expert_body(images, packed_ref, w_in_ref, w_out_ref, act_ref, dhid_ref, back_ref, in_ref, grad_ref,
-                stage_ref, out_acc, back_acc):
+def expert_body(images, packed_ref, w_in_ref, w_out_ref, act_ref, dhid_ref, back_ref,
+                stage_ref, in_ref, grad_ref, out_acc, back_acc):
     f = pl.program_id(0)
     groups = packed_ref.shape[0]
 
@@ -184,18 +184,16 @@
             pl.BlockSpec((rows, block), lambda f: (0, f)),
             pl.BlockSpec((rows, block), lambda f: (0, f)),
             pl.BlockSpec(packed.shape, lambda f: (0, 0, 0)),
-            pl.BlockSpec((rows, width), lambda f: (0, 0)),
-            pl.BlockSpec((rows, width), lambda f: (0, 0)),
         ],
         out_shape=[
             jax.ShapeDtypeStruct((rows, hidden), BF16),
             jax.ShapeDtypeStruct((rows, hidden), BF16),
             jax.ShapeDtypeStruct(packed.shape, BF16),
-            jax.ShapeDtypeStruct((rows, width), BF16),
-            jax.ShapeDtypeStruct((rows, width), BF16),
         ],
         scratch_shapes=[
             stage_shape(packed.shape),
+            pltpu.VMEM((rows, width), BF16),
+            pltpu.VMEM((rows, width), BF16),
             pltpu.VMEM((rows, width), F32),
             pltpu.VMEM((rows, width), F32),
         ],
@@ -296,7 +294,7 @@
         ],
         out_specs=pl.BlockSpec((each, toks, width), image),
         out_shape=jax.ShapeDtypeStruct((images, toks, width), BF16),
-        compiler_params=params(),
+        compiler_params=params(60 * 2**20),
         name="token_grads",
     )(lgrad, dispatch, slot_back, router)
 
@@ -307,7 +305,7 @@
     (w_in_ref, w_out_ref), refs = refs[:2], refs[2:]
     own_refs, refs = refs[:n_own], refs[n_own:]
     first_refs, refs = refs[:n_first], refs[n_first:]
-    gin_ref, gout_ref, stage_ref, in_ref, grad_ref = refs
+    gin_ref, gout_ref, stage_ref, in_ref, grad_ref = refs[:5]
     groups = sum(packed_ref.shape[0] for packed_ref in packed_refs)
 
     @pl.when(pl.program_id(0) == 0)
@@ -315,13 +313,20 @@
         stage_rows(packed_refs, stage_ref)
         load_rows(stage_ref, in_ref, 0, 0, images, groups)
         load_rows(stage_ref, grad_ref, 0, 1, images, groups)
+        if n_own:
+            own_stage_ref, own_in_ref, own_grad_ref = refs[5:]
+            own_groups = own_refs[0].shape[0]
+            stage_rows(own_refs[:1], own_stage_ref)
+            load_rows(own_stage_ref, own_in_ref, 0, 0, images, own_groups)
+            load_rows(own_stage_ref, own_grad_ref, 0, 1, images, own_groups)
 
     act, slope = gelu_parts(mm(in_ref[...], w_in_ref[0], NN))
     dhid = (mm(grad_ref[...], w_out_ref[0], NT) * slope).astype(BF16)
     gin = mm(in_ref[...], dhid, TN)
     gout = mm(act.astype(BF16), grad_ref[...], TN)
     if n_own:
-        own_in_ref, own_grad_ref, own_act_ref, own_dhid_ref = own_refs
+        own_in_ref, own_grad_ref = refs[6:]
+        _, own_act_ref, own_dhid_ref = own_refs
         gin += mm(own_in_ref[...], own_dhid_ref[...], TN)
         gout += mm(own_act_ref[...], own_grad_ref[...], TN)
     if n_first:
@@ -342,8 +347,8 @@
         pl.BlockSpec((1, block, width), lambda f, s: (0, s[0] + f, 0)),
     ]
     if own:
-        own_rows = own[0].shape[0]
-        in_specs += [pl.BlockSpec((own_rows, width), lambda f, s: (0, 0))] * 2
+        own_rows = own[1].shape[0]
+        in_specs += [pl.BlockSpec(own[0].shape, lambda f, s: (0, 0, 0))]
         in_specs += [pl.BlockSpec((own_rows, block), lambda f, s: (0, s[0] + f))] * 2
     outs = [
         pl.BlockSpec((1, width, block), lambda f, s: (0, 0, f)),
@@ -351,6 +356,9 @@
     ]
     if first:
         in_specs += outs
+    scratch = [stage_shape((groups, pieces)), pltpu.VMEM((rows, width), BF16), pltpu.VMEM((rows, width), BF16)]
+    if own:
+        scratch += [stage_shape(own[0].shape)] + [pltpu.VMEM((own_rows, width), BF16)] * 2
     return pl.pallas_call(
         functools.partial(weight_body, images, len(packed), len(own), len(first)),
         grid_spec=pltpu.PrefetchScalarGridSpec(
@@ -358,11 +366,7 @@
             grid=(hidden // block,),
             in_specs=in_specs,
             out_specs=outs,
-            scratch_shapes=[
-                stage_shape((groups, pieces)),
-                pltpu.VMEM((rows, width), BF16),
-                pltpu.VMEM((rows, width), BF16),
-            ],
+            scratch_shapes=scratch,
         ),
         out_shape=[
             jax.ShapeDtypeStruct((1, width, hidden), dtype),
@@ -383,17 +387,16 @@
     slots, width = router.shape
     dispatch, combine, to_experts = gather_slots(tokens, out_grad, router, 3)
     own = swap(to_experts, "exp")
-    act, dhid, to_images, row_in, row_grad = experts(own, w_in, w_out, 512)
+    act, dhid, to_images = experts(own, w_in, w_out, 512)
     hidden, block = w_in.shape[2] // reps, 640
     start = (lax.axis_index("rep") * (hidden // block)).astype(jnp.int32).reshape(1)
     pairs = [(i, i ^ 1) for i in range(reps)]
-    cut = own.shape[0] * 3 // 8
+    cut = own.shape[0] * 7 // 16
     peer_first = lax.ppermute(own[:cut], "rep", pairs)
     peer_last = lax.ppermute(own[cut:], "rep", pairs)
     to_images, peer_first = lax.optimization_barrier((to_images, peer_first))
     back = swap(to_images, "exp")
-    own_rows = (row_in, row_grad, act, dhid)
-    first = weight_grads(start, [peer_first], w_in, w_out, own_rows, (), block, reps, F32, "weight_first")
+    first = weight_grads(start, [peer_first], w_in, w_out, (own, act, dhid), (), block, reps, BF16, "weight_first")
     back, first = lax.optimization_barrier((back, first))
     lgrad, slot_back, tiles = logit_grads(back, tokens, out_grad, dispatch, combine, devices, 2)
     start, tiles = lax.optimization_barrier((start, tiles))

time: 152 us -> 149 us (0.980)
  Pallas kernels: 65.3 us -> 62.4 us
  waiting for transfers between devices: 20.6 us -> 18.9 us
    all_to_all x3, waiting for transfers between devices: 20.6 us -> 17.8 us  [swap(): return lax.all_to_all(value, axis, split_axis=0, concat_axis=0, tiled=True)]
    pallas_call x2, Pallas kernels: 25.8 us -> 23.5 us  [weight_grads(): pl.pallas_call(functools.partial(weight_body, images, len(packed), len(ow...]
  transfers between devices with their start and end apart: 5 -> 5, of which waited for: 2 -> 4; matrix products, arithmetic and copies ran while one was open for 1% -> 1% of each run, Pallas kernels for 38% -> 37%
where the time goes in v2:
time: 149 us
  Pallas kernels  62.4 us (42%)
  blocking collectives  37.9 us (25%)
  starting transfers between devices  25.4 us (17%)
  waiting for transfers between devices  18.9 us (13%)
  local copies, waits for them, and re-layouts  2.79 us (2%)
    all_to_all x1, blocking collectives, swap(): return lax.all_to_all(value, axis, split_axis=0, concat_axis=0, tiled=True)  37.9 us
    pallas_call x2, Pallas kernels, weight_grads(): pl.pallas_call(functools.partial(weight_body, images, len(packed), len(ow...  23.5 us
    all_to_all x3, starting transfers between devices, swap(): return lax.all_to_all(value, axis, split_axis=0, concat_axis=0, tiled=True)  20 us
    all_to_all x3, waiting for transfers between devices, swap(): return lax.all_to_all(value, axis, split_axis=0, concat_axis=0, tiled=True)  17.8 us
    pallas_call x1, Pallas kernels, experts(): pl.pallas_call(functools.partial(expert_body, rows // groups), grid=(hidd...  17.5 us
    pallas_call x1, Pallas kernels, logit_grads(): pl.pallas_call(functools.partial(logit_body, images), grid=(images // eac...  9.4 us
    pallas_call x1, Pallas kernels, gather_slots(): pl.pallas_call(functools.partial(gather_body, images), grid=(images // ea...  7.9 us
    pallas_call x1, Pallas kernels, token_grads(): pl.pallas_call(token_body, grid=(images // each,), in_specs=[pl.BlockSpec...  4 us
  transfers between devices with their start and end apart: 5, of which 4 were waited for; matrix products, arithmetic and copies ran while one was open for 1% of the time, Pallas kernels for 37%

profile of v2, /device:TPU:1, one launch (start us, length us, event | category | flops | bytes accessed | tf_op | source)
XLA Modules:
  0.0 149.0 jit_solution(6019983791131115683)
XLA Ops:
  0.6 7.9 %gather_slots.1 = (f32[6,64,256]{2,1,0:T(8,128)}, f32[6,64,256]{2,1,0:T(8,128)}, bf16[64,120,128]{2,1,0:T(8,128)(2,1)}) custom-call(bf16[6,256,1280]{2,1,0:T(8,128)(2,1)} %tokens_ref.3, bf16[6,256,1280]{2,1,0:T(8,128)(2,1)} %grad_ref.3, bf16[64,1280]{1,0:T(8,128)(2,1)} %router_ref.3), custom_call_target="tpu_custom_call" | custom-call | tf_op jit(solution)/shard_map/gather_slots/pallas_call | solution.py:116
  8.5 37.9 %all_to_all.20.packed_ref.refs_3_ = bf16[64,120,128]{2,1,0:T(8,128)(2,1)S(1)} all-to-all(bf16[64,120,128]{2,1,0:T(8,128)(2,1)} %get-tuple-element.28), channel_id=1, replica_groups=mesh['exp'=64,'rep'=2] {'exp'}, dimensions={0} | all-to-all | bytes 3932160 | tf_op jit(solution)/shard_map/all_to_all | solution.py:381
  46.4 0.0 copy-start
  46.4 0.1 slice.12
  46.5 2.7 %collective-permute-start = (bf16[28,120,128]{2,1,0:T(8,128)(2,1)S(1)}, bf16[28,120,128]{2,1,0:T(8,128)(2,1)S(1)}, u32[]{:S(2)}, u32[]{:S(2)}) collective-permute-start(bf16[28,120,128]{2,1,0:T(8,128)(2,1)S(1)} %slice.12), channel_id=1, source_target_pairs={{0,1},{1,0},{2,3},{3,2},{4,5},{5,4},{6,7},{7,6},{8,9},{9,8},{10,11... | collective-permute-start | bytes 2580488 | tf_op jit(solution)/shard_map/ppermute | solution.py:395
  49.2 0.0 copy-done
  49.2 17.5 %experts.1 = (bf16[384,2560]{1,0:T(8,128)(2,1)}, bf16[384,2560]{1,0:T(8,128)(2,1)}, bf16[64,120,128]{2,1,0:T(8,128)(2,1)}) custom-call(bf16[64,120,128]{2,1,0:T(8,128)(2,1)} %copy-done, bf16[1,1280,2560]{2,1,0:T(8,128)(2,1)} %refs_1_.3, bf16[1,2560,1280]{2,1,0:T(8,128)(2,1)} %refs_2_.3), custom_call_target="tpu_custom_call" | custom-call | tf_op jit(solution)/shard_map/experts/pallas_call | solution.py:175
  66.7 0.0 copy-start.1
  66.7 1.1 collective-permute-done.refs_0_
  67.8 0.0 copy-start.3
  67.8 0.9 copy-done.3
  68.8 6.7 %all-to-all-start.1 = ((bf16[64,120,128]{2,1,0:T(8,128)(2,1)}), bf16[64,120,128]{2,1,0:T(8,128)(2,1)}, u32[]{:S(2)}, u32[]{:S(2)}) async-start(bf16[64,120,128]{2,1,0:T(8,128)(2,1)} %get-tuple-element.30), calls=%async_computation.1 | async-start | bytes 3932160 | tf_op jit(solution)/shard_map/all_to_all | solution.py:381
  75.5 0.0 copy-done.1
  75.5 0.1 slice.13
  75.6 2.7 %collective-permute-start.1 = (bf16[36,120,128]{2,1,0:T(8,128)(2,1)S(1)}, bf16[36,120,128]{2,1,0:T(8,128)(2,1)S(1)}, u32[]{:S(2)}, u32[]{:S(2)}) collective-permute-start(bf16[36,120,128]{2,1,0:T(8,128)(2,1)S(1)} %slice.13), channel_id=1, source_target_pairs={{0,1},{1,0},{2,3},{3,2},{4,5},{5,4},{6,7},{7,6},{8,9},{9,8},{10,11... | collective-permute-start | bytes 3317768 | tf_op jit(solution)/shard_map/ppermute | solution.py:396
  78.3 13.9 %weight_first.1 = (bf16[1,1280,1280]{2,1,0:T(8,128)(2,1)}, bf16[1,1280,1280]{2,1,0:T(8,128)(2,1)}) custom-call(s32[1]{0:T(128)} %bitcast.start_ref, bf16[28,120,128]{2,1,0:T(8,128)(2,1)} %copy-done.3, bf16[1,1280,2560]{2,1,0:T(8,128)(2,1)} %refs_1_.3, bf16[1,2560,1280]{2,1,0:T(8,128)(2,1)} %refs_2_.3, bf16[64,120,128]{2,1,0:T(8,128)(2,1)} %copy-done, ...), custom_call_target="tpu_custom_call" | custom-call | tf_op jit(solution)/shard_map/weight_first/pallas_call | solution.py:362
  92.1 10.4 %all-to-all-done.1.packed_ref = bf16[64,120,128]{2,1,0:T(8,128)(2,1)} async-done(((bf16[64,120,128]{2,1,0:T(8,128)(2,1)}), bf16[64,120,128]{2,1,0:T(8,128)(2,1)}, u32[]{:S(2)}, u32[]{:S(2)}) %all-to-all-start.1) | async-done | bytes 1966112 | tf_op jit(solution)/shard_map/all_to_all | solution.py:381
  102.6 9.4 %logit_grads.1 = (bf16[6,64,256]{2,1,0:T(8,128)(2,1)}, bf16[6,64,1280]{2,1,0:T(8,128)(2,1)}, bf16[128,8,128]{2,1,0:T(8,128)(2,1)}) custom-call(bf16[64,120,128]{2,1,0:T(8,128)(2,1)} %all-to-all-done.1.packed_ref, bf16[6,256,1280]{2,1,0:T(8,128)(2,1)} %tokens_ref.3, bf16[6,256,1280]{2,1,0:T(8,128)(2,1)} %grad_ref.3, ...), custom_call_target="tpu_custom_call" | custom-call | tf_op jit(solution)/shard_map/logit_grads/pallas_call | solution.py:246
  112.0 6.8 %all-to-all-start.2 = ((bf16[128,8,128]{2,1,0:T(8,128)(2,1)}), bf16[128,8,128]{2,1,0:T(8,128)(2,1)S(1)}, u32[]{:S(2)}, u32[]{:S(2)}) async-start(bf16[128,8,128]{2,1,0:T(8,128)(2,1)} %get-tuple-element.40), calls=%async_computation.2 | async-start | bytes 524288 | tf_op jit(solution)/shard_map/all_to_all | solution.py:381
  118.8 4.0 %token_grads.1 = bf16[6,256,1280]{2,1,0:T(8,128)(2,1)} custom-call(bf16[6,64,256]{2,1,0:T(8,128)(2,1)} %get-tuple-element.41.lgrad_ref, f32[6,64,256]{2,1,0:T(8,128)} %get-tuple-element.37.disp_ref, bf16[6,64,1280]{2,1,0:T(8,128)(2,1)} %get-tuple-element.42.sback_ref, bf16[64,1280]{1,0:T(8,128)(2,1)} %router_ref.3), custom_call_target="tpu_custom_call" | custom-call | tf_op jit(solution)/shard_map/token_grads/pallas_call | solution.py:286
  122.8 7.0 %all-to-all-done.2 = bf16[128,8,128]{2,1,0:T(8,128)(2,1)S(1)} async-done(((bf16[128,8,128]{2,1,0:T(8,128)(2,1)}), bf16[128,8,128]{2,1,0:T(8,128)(2,1)S(1)}, u32[]{:S(2)}, u32[]{:S(2)}) %all-to-all-start.2) | async-done | bytes 262176 | tf_op jit(solution)/shard_map/all_to_all | solution.py:381
  129.8 0.1 reduce_sum.12
  129.9 0.7 broadcast_in_dim.2
  130.7 6.5 %all-to-all-start.3 = ((bf16[128,8,128]{2,1,0:T(8,128)(2,1)}), bf16[128,8,128]{2,1,0:T(8,128)(2,1)S(1)}, u32[]{:S(2)}, u32[]{:S(2)}) async-start(bf16[128,8,128]{2,1,0:T(8,128)(2,1)} %broadcast_in_dim.2), calls=%async_computation.3 | async-start | bytes 524288 | tf_op jit(solution)/shard_map/all_to_all | solution.py:381
  137.2 0.0 collective-permute-done.1.refs_0_
  137.2 0.0 copy-start.2
  137.2 1.0 copy-done.2
  138.2 9.7 %weight_last.1 = (bf16[1,1280,1280]{2,1,0:T(8,128)(2,1)}, bf16[1,1280,1280]{2,1,0:T(8,128)(2,1)}) custom-call(s32[1]{0:T(128)} %bitcast.start_ref, bf16[36,120,128]{2,1,0:T(8,128)(2,1)} %copy-done.2, bf16[1,1280,2560]{2,1,0:T(8,128)(2,1)} %refs_1_.3, bf16[1,2560,1280]{2,1,0:T(8,128)(2,1)} %refs_2_.3, bf16[1,1280,1280]{2,1,0:T(8,128)(2,1)} %get-tuple-element.47.refs_3_, ...), custom_call_target="tpu_custom_call" | custom-call | tf_op jit(solution)/shard_map/weight_last/pallas_call | solution.py:362
  147.9 0.3 all-to-all-done.3
  148.2 0.7 convert_bitcast_fusion
  (1 shorter events, 0.0 us)
Async XLA Ops:
  46.4 2.8 %copy-start = (bf16[64,120,128]{2,1,0:T(8,128)(2,1)}, bf16[64,120,128]{2,1,0:T(8,128)(2,1)S(1)}, u32[]{:S(2)}) copy-start(bf16[64,120,128]{2,1,0:T(8,128)(2,1)S(1)} %all_to_all.20.packed_ref.refs_3_) | copy-start | bytes 5898244
  46.5 21.3 %collective-permute-start = (bf16[28,120,128]{2,1,0:T(8,128)(2,1)S(1)}, bf16[28,120,128]{2,1,0:T(8,128)(2,1)S(1)}, u32[]{:S(2)}, u32[]{:S(2)}) collective-permute-start(bf16[28,120,128]{2,1,0:T(8,128)(2,1)S(1)} %slice.12), channel_id=1, source_target_pairs={{0,1},{1,0},{2,3},{3,2},{4,5},{5,4},{6,7},{7,6},{8,9},{9,8},{10,11... | collective-permute-start | bytes 2580488 | tf_op jit(solution)/shard_map/ppermute | solution.py:395
  66.7 8.7 %copy-start.1 = (bf16[64,120,128]{2,1,0:T(8,128)(2,1)S(1)}, bf16[64,120,128]{2,1,0:T(8,128)(2,1)}, u32[]{:S(2)}) copy-start(bf16[64,120,128]{2,1,0:T(8,128)(2,1)} %copy-done) | copy-start | bytes 5898244
  67.8 0.9 copy-start.3
  68.8 33.8 %all-to-all-start.1 = ((bf16[64,120,128]{2,1,0:T(8,128)(2,1)}), bf16[64,120,128]{2,1,0:T(8,128)(2,1)}, u32[]{:S(2)}, u32[]{:S(2)}) async-start(bf16[64,120,128]{2,1,0:T(8,128)(2,1)} %get-tuple-element.30), calls=%async_computation.1 | async-start | bytes 3932160 | tf_op jit(solution)/shard_map/all_to_all | solution.py:381
  75.6 61.6 %collective-permute-start.1 = (bf16[36,120,128]{2,1,0:T(8,128)(2,1)S(1)}, bf16[36,120,128]{2,1,0:T(8,128)(2,1)S(1)}, u32[]{:S(2)}, u32[]{:S(2)}) collective-permute-start(bf16[36,120,128]{2,1,0:T(8,128)(2,1)S(1)} %slice.13), channel_id=1, source_target_pairs={{0,1},{1,0},{2,3},{3,2},{4,5},{5,4},{6,7},{7,6},{8,9},{9,8},{10,11... | collective-permute-start | bytes 3317768 | tf_op jit(solution)/shard_map/ppermute | solution.py:396
  112.0 17.8 %all-to-all-start.2 = ((bf16[128,8,128]{2,1,0:T(8,128)(2,1)}), bf16[128,8,128]{2,1,0:T(8,128)(2,1)S(1)}, u32[]{:S(2)}, u32[]{:S(2)}) async-start(bf16[128,8,128]{2,1,0:T(8,128)(2,1)} %get-tuple-element.40), calls=%async_computation.2 | async-start | bytes 524288 | tf_op jit(solution)/shard_map/all_to_all | solution.py:381
  130.7 17.5 %all-to-all-start.3 = ((bf16[128,8,128]{2,1,0:T(8,128)(2,1)}), bf16[128,8,128]{2,1,0:T(8,128)(2,1)S(1)}, u32[]{:S(2)}, u32[]{:S(2)}) async-start(bf16[128,8,128]{2,1,0:T(8,128)(2,1)} %broadcast_in_dim.2), calls=%async_computation.3 | async-start | bytes 524288 | tf_op jit(solution)/shard_map/all_to_all | solution.py:381
  137.2 1.0 copy-start.2

commit v3 on v2

--- a/solution.py
+++ b/solution.py
@@ -294,7 +294,7 @@
         ],
         out_specs=pl.BlockSpec((each, toks, width), image),
         out_shape=jax.ShapeDtypeStruct((images, toks, width), BF16),
-        compiler_params=params(60 * 2**20),
+        compiler_params=params(127 * 2**19),
         name="token_grads",
     )(lgrad, dispatch, slot_back, router)
 

time: 149 us -> 149 us (level)
    unnamed x8 -> x6, local copies, waits for them, and re-layouts: 1.9 us -> 0.01 us
where the time goes in v3:
time: 149 us; the launch traced here: 148 us
  Pallas kernels  62.3 us (42%)
  blocking collectives  37.9 us (25%)
  starting transfers between devices  25.3 us (17%)
  waiting for transfers between devices  19 us (13%)
  local copies, waits for them, and re-layouts  1.91 us (1%)
    all_to_all x1, blocking collectives, swap(): return lax.all_to_all(value, axis, split_axis=0, concat_axis=0, tiled=True)  37.9 us
    pallas_call x2, Pallas kernels, weight_grads(): pl.pallas_call(functools.partial(weight_body, images, len(packed), len(ow...  23.5 us
    all_to_all x3, starting transfers between devices, swap(): return lax.all_to_all(value, axis, split_axis=0, concat_axis=0, tiled=True)  20 us
    all_to_all x3, waiting for transfers between devices, swap(): return lax.all_to_all(value, axis, split_axis=0, concat_axis=0, tiled=True)  17.8 us
    pallas_call x1, Pallas kernels, experts(): pl.pallas_call(functools.partial(expert_body, rows // groups), grid=(hidd...  17.5 us
    pallas_call x1, Pallas kernels, logit_grads(): pl.pallas_call(functools.partial(logit_body, images), grid=(images // eac...  9.4 us
    pallas_call x1, Pallas kernels, gather_slots(): pl.pallas_call(functools.partial(gather_body, images), grid=(images // ea...  7.9 us
    pallas_call x1, Pallas kernels, token_grads(): pl.pallas_call(token_body, grid=(images // each,), in_specs=[pl.BlockSpec...  4 us
  transfers between devices with their start and end apart: 5, of which 4 were waited for; matrix products, arithmetic and copies ran while one was open for 1% of the time, Pallas kernels for 37%

profile of v3, /device:TPU:1, one launch (start us, length us, event | category | flops | bytes accessed | tf_op | source)
XLA Modules:
  0.0 148.0 jit_solution(16248067795145373466)
XLA Ops:
  0.6 7.9 %gather_slots.1 = (f32[6,64,256]{2,1,0:T(8,128)}, f32[6,64,256]{2,1,0:T(8,128)}, bf16[64,120,128]{2,1,0:T(8,128)(2,1)}) custom-call(bf16[6,256,1280]{2,1,0:T(8,128)(2,1)} %tokens_ref.3, bf16[6,256,1280]{2,1,0:T(8,128)(2,1)} %grad_ref.3, bf16[64,1280]{1,0:T(8,128)(2,1)} %router_ref.3), custom_call_target="tpu_custom_call" | custom-call | tf_op jit(solution)/shard_map/gather_slots/pallas_call | solution.py:116
  8.5 37.9 %all_to_all.20.packed_ref.refs_3_ = bf16[64,120,128]{2,1,0:T(8,128)(2,1)S(1)} all-to-all(bf16[64,120,128]{2,1,0:T(8,128)(2,1)} %get-tuple-element.28), channel_id=1, replica_groups=mesh['exp'=64,'rep'=2] {'exp'}, dimensions={0} | all-to-all | bytes 3932160 | tf_op jit(solution)/shard_map/all_to_all | solution.py:381
  46.4 0.0 copy-start
  46.4 0.1 slice.12
  46.5 2.7 %collective-permute-start = (bf16[28,120,128]{2,1,0:T(8,128)(2,1)S(1)}, bf16[28,120,128]{2,1,0:T(8,128)(2,1)S(1)}, u32[]{:S(2)}, u32[]{:S(2)}) collective-permute-start(bf16[28,120,128]{2,1,0:T(8,128)(2,1)S(1)} %slice.12), channel_id=1, source_target_pairs={{0,1},{1,0},{2,3},{3,2},{4,5},{5,4},{6,7},{7,6},{8,9},{9,8},{10,11... | collective-permute-start | bytes 2580488 | tf_op jit(solution)/shard_map/ppermute | solution.py:395
  49.2 0.0 copy-done
  49.2 17.5 %experts.1 = (bf16[384,2560]{1,0:T(8,128)(2,1)}, bf16[384,2560]{1,0:T(8,128)(2,1)}, bf16[64,120,128]{2,1,0:T(8,128)(2,1)}) custom-call(bf16[64,120,128]{2,1,0:T(8,128)(2,1)} %copy-done, bf16[1,1280,2560]{2,1,0:T(8,128)(2,1)} %refs_1_.3, bf16[1,2560,1280]{2,1,0:T(8,128)(2,1)} %refs_2_.3), custom_call_target="tpu_custom_call" | custom-call | tf_op jit(solution)/shard_map/experts/pallas_call | solution.py:175
  66.7 0.0 copy-start.1
  66.7 1.1 collective-permute-done.refs_0_
  67.8 0.0 copy-start.2
  67.8 6.7 %all-to-all-start.1 = ((bf16[64,120,128]{2,1,0:T(8,128)(2,1)}), bf16[64,120,128]{2,1,0:T(8,128)(2,1)}, u32[]{:S(2)}, u32[]{:S(2)}) async-start(bf16[64,120,128]{2,1,0:T(8,128)(2,1)} %get-tuple-element.30), calls=%async_computation.1 | async-start | bytes 3932160 | tf_op jit(solution)/shard_map/all_to_all | solution.py:381
  74.5 0.0 copy-done.1
  74.5 1.1 slice.13
  75.6 2.6 %collective-permute-start.1 = (bf16[36,120,128]{2,1,0:T(8,128)(2,1)}, bf16[36,120,128]{2,1,0:T(8,128)(2,1)}, u32[]{:S(2)}, u32[]{:S(2)}) collective-permute-start(bf16[36,120,128]{2,1,0:T(8,128)(2,1)} %slice.13), channel_id=1, source_target_pairs={{0,1},{1,0},{2,3},{3,2},{4,5},{5,4},{6,7},{7,6},{8,9},{9,8},{10,11... | collective-permute-start | bytes 3317768 | tf_op jit(solution)/shard_map/ppermute | solution.py:396
  78.2 0.0 copy-done.2
  78.2 13.9 %weight_first.1 = (bf16[1,1280,1280]{2,1,0:T(8,128)(2,1)}, bf16[1,1280,1280]{2,1,0:T(8,128)(2,1)}) custom-call(s32[1]{0:T(128)} %bitcast.start_ref, bf16[28,120,128]{2,1,0:T(8,128)(2,1)} %copy-done.2, bf16[1,1280,2560]{2,1,0:T(8,128)(2,1)} %refs_1_.3, bf16[1,2560,1280]{2,1,0:T(8,128)(2,1)} %refs_2_.3, bf16[64,120,128]{2,1,0:T(8,128)(2,1)} %copy-done, ...), custom_call_target="tpu_custom_call" | custom-call | tf_op jit(solution)/shard_map/weight_first/pallas_call | solution.py:362
  92.1 9.5 %all-to-all-done.1.packed_ref = bf16[64,120,128]{2,1,0:T(8,128)(2,1)} async-done(((bf16[64,120,128]{2,1,0:T(8,128)(2,1)}), bf16[64,120,128]{2,1,0:T(8,128)(2,1)}, u32[]{:S(2)}, u32[]{:S(2)}) %all-to-all-start.1) | async-done | bytes 1966112 | tf_op jit(solution)/shard_map/all_to_all | solution.py:381
  101.6 9.4 %logit_grads.1 = (bf16[6,64,256]{2,1,0:T(8,128)(2,1)}, bf16[6,64,1280]{2,1,0:T(8,128)(2,1)}, bf16[128,8,128]{2,1,0:T(8,128)(2,1)}) custom-call(bf16[64,120,128]{2,1,0:T(8,128)(2,1)} %all-to-all-done.1.packed_ref, bf16[6,256,1280]{2,1,0:T(8,128)(2,1)} %tokens_ref.3, bf16[6,256,1280]{2,1,0:T(8,128)(2,1)} %grad_ref.3, ...), custom_call_target="tpu_custom_call" | custom-call | tf_op jit(solution)/shard_map/logit_grads/pallas_call | solution.py:246
  111.0 6.8 %all-to-all-start.2 = ((bf16[128,8,128]{2,1,0:T(8,128)(2,1)}), bf16[128,8,128]{2,1,0:T(8,128)(2,1)S(1)}, u32[]{:S(2)}, u32[]{:S(2)}) async-start(bf16[128,8,128]{2,1,0:T(8,128)(2,1)} %get-tuple-element.40), calls=%async_computation.2 | async-start | bytes 524288 | tf_op jit(solution)/shard_map/all_to_all | solution.py:381
  117.9 4.0 %token_grads.1 = bf16[6,256,1280]{2,1,0:T(8,128)(2,1)} custom-call(bf16[6,64,256]{2,1,0:T(8,128)(2,1)} %get-tuple-element.41.lgrad_ref, f32[6,64,256]{2,1,0:T(8,128)} %get-tuple-element.37.disp_ref, bf16[6,64,1280]{2,1,0:T(8,128)(2,1)} %get-tuple-element.42.sback_ref, bf16[64,1280]{1,0:T(8,128)(2,1)} %router_ref.3), custom_call_target="tpu_custom_call" | custom-call | tf_op jit(solution)/shard_map/token_grads/pallas_call | solution.py:286
  121.9 7.0 %all-to-all-done.2 = bf16[128,8,128]{2,1,0:T(8,128)(2,1)S(1)} async-done(((bf16[128,8,128]{2,1,0:T(8,128)(2,1)}), bf16[128,8,128]{2,1,0:T(8,128)(2,1)S(1)}, u32[]{:S(2)}, u32[]{:S(2)}) %all-to-all-start.2) | async-done | bytes 262176 | tf_op jit(solution)/shard_map/all_to_all | solution.py:381
  128.9 0.1 reduce_sum.12
  129.0 0.7 broadcast_in_dim.2
  129.8 6.5 %all-to-all-start.3 = ((bf16[128,8,128]{2,1,0:T(8,128)(2,1)}), bf16[128,8,128]{2,1,0:T(8,128)(2,1)S(1)}, u32[]{:S(2)}, u32[]{:S(2)}) async-start(bf16[128,8,128]{2,1,0:T(8,128)(2,1)} %broadcast_in_dim.2), calls=%async_computation.3 | async-start | bytes 524288 | tf_op jit(solution)/shard_map/all_to_all | solution.py:381
  136.3 0.0 collective-permute-done.1.refs_0_
  136.3 9.7 %weight_last.1 = (bf16[1,1280,1280]{2,1,0:T(8,128)(2,1)}, bf16[1,1280,1280]{2,1,0:T(8,128)(2,1)}) custom-call(s32[1]{0:T(128)} %bitcast.start_ref, bf16[36,120,128]{2,1,0:T(8,128)(2,1)} %collective-permute-done.1.refs_0_, bf16[1,1280,2560]{2,1,0:T(8,128)(2,1)} %refs_1_.3, bf16[1,2560,1280]{2,1,0:T(8,128)(2,1)} %refs_2_.3, ...), custom_call_target="tpu_custom_call" | custom-call | tf_op jit(solution)/shard_map/weight_last/pallas_call | solution.py:362
  145.9 1.3 all-to-all-done.3
  147.3 0.7 convert_bitcast_fusion
  (1 shorter events, 0.0 us)
Async XLA Ops:
  46.4 2.8 %copy-start = (bf16[64,120,128]{2,1,0:T(8,128)(2,1)}, bf16[64,120,128]{2,1,0:T(8,128)(2,1)S(1)}, u32[]{:S(2)}) copy-start(bf16[64,120,128]{2,1,0:T(8,128)(2,1)S(1)} %all_to_all.20.packed_ref.refs_3_) | copy-start | bytes 5898244
  46.5 21.3 %collective-permute-start = (bf16[28,120,128]{2,1,0:T(8,128)(2,1)S(1)}, bf16[28,120,128]{2,1,0:T(8,128)(2,1)S(1)}, u32[]{:S(2)}, u32[]{:S(2)}) collective-permute-start(bf16[28,120,128]{2,1,0:T(8,128)(2,1)S(1)} %slice.12), channel_id=1, source_target_pairs={{0,1},{1,0},{2,3},{3,2},{4,5},{5,4},{6,7},{7,6},{8,9},{9,8},{10,11... | collective-permute-start | bytes 2580488 | tf_op jit(solution)/shard_map/ppermute | solution.py:395
  66.7 7.8 %copy-start.1 = (bf16[64,120,128]{2,1,0:T(8,128)(2,1)S(1)}, bf16[64,120,128]{2,1,0:T(8,128)(2,1)}, u32[]{:S(2)}) copy-start(bf16[64,120,128]{2,1,0:T(8,128)(2,1)} %copy-done) | copy-start | bytes 5898244
  67.8 10.4 %copy-start.2 = (bf16[28,120,128]{2,1,0:T(8,128)(2,1)}, bf16[28,120,128]{2,1,0:T(8,128)(2,1)S(1)}, u32[]{:S(2)}) copy-start(bf16[28,120,128]{2,1,0:T(8,128)(2,1)S(1)} %collective-permute-done.refs_0_) | copy-start | bytes 2580484
  67.8 33.8 %all-to-all-start.1 = ((bf16[64,120,128]{2,1,0:T(8,128)(2,1)}), bf16[64,120,128]{2,1,0:T(8,128)(2,1)}, u32[]{:S(2)}, u32[]{:S(2)}) async-start(bf16[64,120,128]{2,1,0:T(8,128)(2,1)} %get-tuple-element.30), calls=%async_computation.1 | async-start | bytes 3932160 | tf_op jit(solution)/shard_map/all_to_all | solution.py:381
  75.6 60.6 %collective-permute-start.1 = (bf16[36,120,128]{2,1,0:T(8,128)(2,1)}, bf16[36,120,128]{2,1,0:T(8,128)(2,1)}, u32[]{:S(2)}, u32[]{:S(2)}) collective-permute-start(bf16[36,120,128]{2,1,0:T(8,128)(2,1)} %slice.13), channel_id=1, source_target_pairs={{0,1},{1,0},{2,3},{3,2},{4,5},{5,4},{6,7},{7,6},{8,9},{9,8},{10,11... | collective-permute-start | bytes 3317768 | tf_op jit(solution)/shard_map/ppermute | solution.py:396
  111.0 17.8 %all-to-all-start.2 = ((bf16[128,8,128]{2,1,0:T(8,128)(2,1)}), bf16[128,8,128]{2,1,0:T(8,128)(2,1)S(1)}, u32[]{:S(2)}, u32[]{:S(2)}) async-start(bf16[128,8,128]{2,1,0:T(8,128)(2,1)} %get-tuple-element.40), calls=%async_computation.2 | async-start | bytes 524288 | tf_op jit(solution)/shard_map/all_to_all | solution.py:381
  129.8 17.5 %all-to-all-start.3 = ((bf16[128,8,128]{2,1,0:T(8,128)(2,1)}), bf16[128,8,128]{2,1,0:T(8,128)(2,1)S(1)}, u32[]{:S(2)}, u32[]{:S(2)}) async-start(bf16[128,8,128]{2,1,0:T(8,128)(2,1)} %broadcast_in_dim.2), calls=%async_computation.3 | async-start | bytes 524288 | tf_op jit(solution)/shard_map/all_to_all | solution.py:381
